TPU v7x, 32 devices: a whole 2x2x4 slice. The times are simulated.
32 devices in a mesh: chan: 8 (over z, y), grp: 4 (over x, core).
Axes of the slice: x: 2, y: 2, z: 4, core: 2. Of those that a mesh axis runs over, the one named last changes fastest.
Arguments:
- gate_up: bfloat16 [4096, 2, 28672], P('grp', None, 'chan'), may hold values from -6 to 6
- counts: int32 [4], P('grp'), may hold values from 512 to 1024
- panels: int32 [2, 512], replicated, may hold values from 0 to 28671, as said below
- inverses: float32 [2, 512, 512], replicated
- down_weight: bfloat16 [28672, 8192], P('chan', 'grp'), may hold values from -6 to 6
Outputs:
- pruned_weight: bfloat16 [28672, 8192], P('chan', 'grp')
Inputs may be any that keep to these rules, and one draw needn't show every extreme that they name: `panels`: the entries 512 // 8 * s to 512 // 8 * (s + 1) - 1 of each panel lie in channels s * (28672 // 8) to (s + 1) * (28672 // 8) - 1; all 1024 indices are different.
All inputs are finite; a program needn't handle non-finite values.
Results may differ from a plain program's by a relative error of at most 0.0051.
Values may be sent and summed in bfloat16 or wider, within the bound.
A program may use at most 128 MiB of HBM per device.

v0:
```python
import jax
import jax.numpy as jnp
from jax import lax
from jax.sharding import PartitionSpec as P


def body(gate_up, counts, panels, inverses, down_weight):
    local = gate_up.shape[2]
    share = panels.shape[1] // lax.axis_size("chan")
    shard = lax.axis_index("chan")
    slot = jnp.arange(gate_up.shape[0], dtype=jnp.int32)
    valid = (slot < counts[0]).astype(jnp.float32)
    gate_half = gate_up[:, 0, :].astype(jnp.float32)
    up_half = gate_up[:, 1, :].astype(jnp.float32)
    hidden = (jax.nn.silu(gate_half) * up_half * valid[:, None]).astype(jnp.bfloat16)
    picked = lax.dynamic_slice(panels, (0, shard * share), (2, share)) - shard * local
    first_acts, second_acts = (
        lax.all_gather(jnp.take(hidden, picked[0], axis=1), "chan", axis=1, tiled=True),
        lax.all_gather(jnp.take(hidden, picked[1], axis=1), "chan", axis=1, tiled=True),
    )
    dims = (((0,), (0,)), ((), ()))
    first_part = lax.dot_general(hidden, first_acts, dims, preferred_element_type=jnp.float32)
    second_part = lax.dot_general(hidden, second_acts, dims, preferred_element_type=jnp.float32)
    first_sum, second_sum, total = lax.psum(
        (first_part, second_part, counts[0].astype(jnp.float32)), "grp"
    )
    hessians = (first_sum / total, second_sum / total)
    high = lax.Precision.HIGHEST
    first_rows, second_rows = (
        lax.all_gather(jnp.take(down_weight, picked[0], axis=0), "chan", axis=0, tiled=True),
        lax.all_gather(jnp.take(down_weight, picked[1], axis=0), "chan", axis=0, tiled=True),
    )
    cross = lax.all_gather(jnp.take(hessians[0], picked[1], axis=0), "chan", axis=0, tiled=True)
    first_update = jnp.dot(inverses[0], first_rows.astype(jnp.float32), precision=high)
    second_current = second_rows.astype(jnp.float32) - jnp.dot(cross, first_update, precision=high)
    second_update = jnp.dot(inverses[1], second_current, precision=high)
    joined_hess = jnp.concatenate(hessians, axis=1)
    joined_update = jnp.concatenate((first_update, second_update), axis=0)
    weight_state = down_weight.astype(jnp.float32) - jnp.dot(
        joined_hess, joined_update, precision=high
    )
    weight_state = weight_state.at[picked[0]].set(0.0)
    weight_state = weight_state.at[picked[1]].set(0.0)
    return weight_state.astype(jnp.bfloat16)


def solution(mesh):
    in_specs = (P("grp", None, "chan"), P("grp"), P(), P(), P("chan", "grp"))
    out_specs = P("chan", "grp")
    return jax.shard_map(body, mesh=mesh, in_specs=in_specs, out_specs=out_specs, check_vma=False)
```

profile of v0, /device:TPU:26, one launch (start us, length us, event | category | flops | bytes accessed | tf_op | source)
XLA Modules:
  0.0 772.7 jit_solution(10042167021424888006)
XLA Ops:
  8.0 29.1 %fusion.31 = (bf16[1024,1,3584]{2,1,0:T(2,128)(2,1)}, bf16[1024,1,3584]{2,1,0:T(2,128)(2,1)}) fusion(bf16[1024,2,3584]{2,1,0:T(2,128)(2,1)} %param.9), kind=kLoop, calls=%fused_computation.57 | loop fusion | bytes 29360128 | tf_op jit(solution)/shard_map/slice | solution.py:13
  37.1 30.7 %copy.8 = bf16[1024,1,3584]{0,2,1:T(8,128)(2,1)} copy(bf16[1024,1,3584]{2,1,0:T(2,128)(2,1)} %get-tuple-element.13) | data formatting | bytes 14680064
  67.8 30.6 %copy.9 = bf16[1024,1,3584]{0,2,1:T(8,128)(2,1)} copy(bf16[1024,1,3584]{2,1,0:T(2,128)(2,1)} %get-tuple-element.14) | data formatting | bytes 14680064
  98.3 10.4 %fusion.8 = bf16[1024,3584]{0,1:T(8,128)(2,1)} fusion(bf16[1024,1,3584]{0,2,1:T(8,128)(2,1)} %copy.9, bf16[1024,1,3584]{0,2,1:T(8,128)(2,1)} %copy.8, f32[1024]{0:T(1024)S(1)} %fusion.27), kind=kLoop, calls=%fused_computation.18 | loop fusion | flops 33030144 | bytes 22024192 | tf_op jit(solution)/shard_map/convert_element_type | solution.py:15
  120.2 34.1 %all-gather.6.cloned.1.call-done = bf16[1024,512]{0,1:T(8,128)(2,1)} async-done(((bf16[1024,64]{0,1:T(8,128)(2,1)}), bf16[1024,512]{0,1:T(8,128)(2,1)}) %all-gather.6.cloned.1.call-update) | async-done | bytes 1048592 | tf_op jit(solution)/shard_map/all_gather | solution.py:18
  154.3 10.4 %fusion.32 = f32[3584,512]{1,0:T(8,128)} fusion(bf16[1024,3584]{0,1:T(8,128)(2,1)} %fusion.8, bf16[1024,512]{0,1:T(8,128)(2,1)} %all-gather.6.cloned.1.call-done), kind=kOutput, calls=%fused_computation.58 | convolution fusion | flops 3758096384 | bytes 15728640 | tf_op jit(solution)/shard_map/dot_general | solution.py:22
  164.7 30.7 %all-gather.8.cloned.1.call-done = bf16[1024,512]{0,1:T(8,128)(2,1)} async-done(((bf16[1024,64]{0,1:T(8,128)(2,1)}), bf16[1024,512]{0,1:T(8,128)(2,1)}) %all-gather.8.cloned.1.call-update) | async-done | bytes 1048592 | tf_op jit(solution)/shard_map/all_gather | solution.py:19
  195.4 10.3 %fusion.33 = f32[3584,512]{1,0:T(8,128)} fusion(bf16[1024,3584]{0,1:T(8,128)(2,1)} %fusion.8, bf16[1024,512]{0,1:T(8,128)(2,1)} %all-gather.8.cloned.1.call-done), kind=kOutput, calls=%fused_computation.59 | convolution fusion | flops 3758096384 | bytes 15728640 | tf_op jit(solution)/shard_map/dot_general | solution.py:23
  205.8 8.0 %gather_fusion.3 = bf16[64,2048]{1,0:T(8,128)(2,1)S(1)} fusion(bf16[3584,2048]{1,0:T(8,128)(2,1)} %param.13, s32[1024]{0:T(1024)S(1)} %pad_clamp_fusion.2), kind=kCustom, calls=%fused_computation.1.clone | custom fusion | bytes 524544 | tf_op jit(solution)/shard_map/jit(_take)/gather | solution.py:30
  214.7 6.8 psum.22
  221.5 238.8 %all-reduce.3.cloned.1.call-done = (f32[3584,512]{1,0:T(8,128)}, f32[3584,512]{1,0:T(8,128)}) async-done(((f32[3584,512]{1,0:T(8,128)}, f32[3584,512]{1,0:T(8,128)}), (f32[3584,512]{1,0:T(8,128)}, f32[3584,512]{1,0:T(8,128)})) %all-reduce.3.cloned.1.call-update) | async-done | bytes 14680080 | tf_op jit(solution)/shard_map/psum | solution.py:24
  460.3 7.7 broadcast_divide_fusion.1
  473.1 8.1 %gather_fusion.4 = bf16[64,2048]{1,0:T(8,128)(2,1)S(1)} fusion(bf16[3584,2048]{1,0:T(8,128)(2,1)} %param.13, s32[1024]{0:T(1024)S(1)} %pad_clamp_fusion.1), kind=kCustom, calls=%fused_computation.3.clone | custom fusion | bytes 524544 | tf_op jit(solution)/shard_map/jit(_take)/gather | solution.py:31
  482.0 29.0 %all-gather.10.cloned.1.call-done = bf16[512,2048]{1,0:T(8,128)(2,1)} async-done(((bf16[64,2048]{1,0:T(8,128)(2,1)}), bf16[512,2048]{1,0:T(8,128)(2,1)}) %all-gather.10.cloned.1.call-update) | async-done | bytes 2097168 | tf_op jit(solution)/shard_map/all_gather | solution.py:30
  511.0 6.5 fusion.19
  517.5 7.7 broadcast_divide_fusion
  525.2 26.7 %all-gather.14.cloned.1.call-done = f32[512,512]{1,0:T(8,128)} async-done(((f32[64,512]{1,0:T(8,128)}), f32[512,512]{1,0:T(8,128)}) %all-gather.14.cloned.1.call-update) | async-done | bytes 1048592 | tf_op jit(solution)/shard_map/all_gather | solution.py:33
  551.9 10.3 %fusion.34 = f32[512,2048]{1,0:T(8,128)} fusion(f32[512,512]{1,0:T(8,128)} %all-gather.14.cloned.1.call-done, f32[2048,512]{0,1:T(8,128)} %fusion.19), kind=kOutput, calls=%fused_computation.60 | convolution fusion | flops 6442450944 | bytes 9437184 | tf_op jit(solution)/shard_map/dot_general | solution.py:35
  562.3 39.4 %all-gather.12.cloned.1.call-done = bf16[512,2048]{1,0:T(8,128)(2,1)} async-done(((bf16[64,2048]{1,0:T(8,128)(2,1)}), bf16[512,2048]{1,0:T(8,128)(2,1)}) %all-gather.12.cloned.1.call-update) | async-done | bytes 2097168 | tf_op jit(solution)/shard_map/all_gather | solution.py:31
  601.7 9.1 %fusion.15 = f32[512,2048]{1,0:T(8,128)S(1)} fusion(f32[512,2048]{1,0:T(8,128)} %fusion.34, bf16[512,2048]{1,0:T(8,128)(2,1)} %all-gather.12.cloned.1.call-done, f32[2,512,512]{2,1,0:T(8,128)S(1)} %copy-done.1), kind=kOutput, calls=%fused_computation.27 | convolution fusion | flops 6444548096 | bytes 11534336 | tf_op jit(solution)/shard_map/dot_general | solution.py:36
  610.9 98.5 %convert_subtract_fusion = f32[3584,2048]{1,0:T(8,128)} fusion(bf16[3584,2048]{1,0:T(8,128)(2,1)} %param.13, f32[3584,512]{1,0:T(8,128)} %broadcast_divide_fusion, f32[3584,512]{1,0:T(8,128)} %broadcast_divide_fusion.1, f32[512,2048]{1,0:T(8,128)S(1)} %fusion.15, f32[512,2048]{1,0:T(8,128)S(1)} %bitcast.45), kind=kOutput, calls=%fused_computation.7 | convolution fusion | flops 90214760448 | bytes 67108864 | tf_op jit(solution)/shard_map/dot_general | solution.py:39
  709.4 19.9 %scatter_custom_fusion = f32[3584,2048]{1,0:T(8,128)} fusion(f32[3584,2048]{1,0:T(8,128)} %convert_subtract_fusion, s32[64]{0:T(128)S(1)} %get-tuple-element.15, f32[]{:T(128)} %constant.39.clone.1), kind=kCustom, calls=%fused_computation.35 | custom fusion | bytes 29360640 | tf_op jit(solution)/shard_map/scatter | solution.py:42
  729.3 19.9 %scatter_custom_fusion.1 = f32[3584,2048]{1,0:T(8,128)} fusion(f32[3584,2048]{1,0:T(8,128)} %scatter_custom_fusion, s32[64]{0:T(128)S(1)} %get-tuple-element.16, f32[]{:T(128)} %constant.39.clone.1), kind=kCustom, calls=%fused_computation.33 | custom fusion | bytes 29360640 | tf_op jit(solution)/shard_map/scatter | solution.py:43
  749.2 16.5 %convert_element_type.44 = bf16[3584,2048]{1,0:T(8,128)(2,1)} convert(f32[3584,2048]{1,0:T(8,128)} %scatter_custom_fusion.1) | non-fusion elementwise | flops 7340032 | bytes 44040192 | tf_op jit(solution)/shard_map/convert_element_type | solution.py:44
  (31 shorter events, 19.0 us)
Async XLA Ops:
  6.5 147.8 %all-gather.6.cloned.1.call-start = ((), (), s32[]{:S(2)}) async-start(), calls=%async_computation | async-start | bytes 1179648 | tf_op jit(solution)/shard_map/all_gather | solution.py:18
  114.3 81.1 %all-gather.8.cloned.1.call-start = ((), (), s32[]{:S(2)}) async-start(), calls=%async_computation.1 | async-start | bytes 1179648 | tf_op jit(solution)/shard_map/all_gather | solution.py:19
  120.0 340.3 %all-reduce.3.cloned.1.call-start = ((), (), s32[]{:S(2)}) async-start(), calls=%async_computation.5 | async-start | bytes 29360128 | tf_op jit(solution)/shard_map/psum | solution.py:24
  205.7 305.3 %all-gather.10.cloned.1.call-start = ((), (), s32[]{:S(2)}) async-start(), calls=%async_computation.2 | async-start | bytes 2359296 | tf_op jit(solution)/shard_map/all_gather | solution.py:30
  214.7 337.3 %all-gather.14.cloned.1.call-start = ((), (), s32[]{:S(2)}) async-start(), calls=%async_computation.4 | async-start | bytes 1179648 | tf_op jit(solution)/shard_map/all_gather | solution.py:33
  460.3 50.7 %copy-start.1 = (f32[2,512,512]{2,1,0:T(8,128)S(1)}, f32[2,512,512]{2,1,0:T(8,128)}, u32[]{:S(2)}) copy-start(f32[2,512,512]{2,1,0:T(8,128)} %param.12) | copy-start | bytes 6291460
  472.6 129.1 %all-gather.12.cloned.1.call-start = ((), (), s32[]{:S(2)}) async-start(), calls=%async_computation.3 | async-start | bytes 2359296 | tf_op jit(solution)/shard_map/all_gather | solution.py:31
  601.7 9.2 %copy-start = (f32[2048,512]{0,1:T(8,128)S(1)}, f32[2048,512]{0,1:T(8,128)}, u32[]{:S(2)}) copy-start(f32[2048,512]{0,1:T(8,128)} %fusion.19) | copy-start | bytes 12582916
Sparse Core Ops, SparseCore 0:
  114.5 39.8 all-gather.5
  156.5 38.8 all-gather.7
  205.8 254.4 all-reduce.2
  462.3 48.6 all-gather.9
  513.0 38.8 all-gather.13
  553.9 47.7 all-gather.11
where the time goes:
time: 783 us; the launch traced here: 773 us
  waiting for transfers between devices  399 us (51%)
  local copies, waits for them, and re-layouts  160 us (20%)
  matrix products  145 us (19%)
  other arithmetic  46.9 us (6%)
  between operations  14.4 us (2%)
    psum x1, waiting for transfers between devices, body(): lax.psum((first_part, second_part, counts[0].astype(jnp.float32)), 'grp')  239 us
    dot_general x1, matrix products, body(): jnp.dot(joined_hess, joined_update, precision=high)  98.5 us
    unnamed x6, local copies, waits for them, and re-layouts  61.3 us
    all_gather x1, waiting for transfers between devices, body(): lax.all_gather(jnp.take(down_weight, picked[1], axis=0), 'chan', axis=0,...  39.4 us
    all_gather x1, waiting for transfers between devices, body(): lax.all_gather(jnp.take(hidden, picked[0], axis=1), 'chan', axis=1, tiled...  34.1 us
    all_gather x1, waiting for transfers between devices, body(): lax.all_gather(jnp.take(hidden, picked[1], axis=1), 'chan', axis=1, tiled...  30.7 us
    slice x1, local copies, waits for them, and re-layouts, body(): gate_half = gate_up[:, 0, :].astype(jnp.float32)  29.1 us
    all_gather x1, waiting for transfers between devices, body(): lax.all_gather(jnp.take(down_weight, picked[0], axis=0), 'chan', axis=0,...  29 us
  transfers between devices with their start and end apart: 6, of which 6 were waited for; matrix products, arithmetic and copies ran while one was open for 9% of the time, Pallas kernels for 0%

commit v1 on v0

v1 whole, which is shorter than its diff:
```python
import functools

import jax
import jax.numpy as jnp
from jax import lax
from jax.experimental import pallas as pl
from jax.experimental.pallas import tpu as pltpu
from jax.sharding import PartitionSpec as P

MESH = pl.DeviceIdType.MESH
NT = (((1,), (1,)), ((), ()))


def hidden_kernel(count_ref, x_ref, pick_ref, hidden_ref, acts_ref):
    rows = x_ref.shape[0]
    pairs = x_ref[...].reshape(2 * rows, x_ref.shape[2])
    row = lax.broadcasted_iota(jnp.int32, (rows, 2 * rows), 0)
    col = lax.broadcasted_iota(jnp.int32, (rows, 2 * rows), 1)
    gate = jnp.dot((col == 2 * row).astype(jnp.bfloat16), pairs, preferred_element_type=jnp.float32)
    up = jnp.dot((col == 2 * row + 1).astype(jnp.bfloat16), pairs, preferred_element_type=jnp.float32)
    slot = lax.broadcasted_iota(jnp.int32, (rows, 1), 0) + pl.program_id(0) * rows
    valid = (slot < count_ref[0]).astype(jnp.float32)
    hidden = (gate / (1.0 + jnp.exp(-gate)) * up * valid).astype(jnp.bfloat16)
    hidden_ref[...] = hidden
    acts_ref[...] = lax.dot_general(
        pick_ref[...], hidden, NT, preferred_element_type=jnp.float32
    ).astype(jnp.bfloat16)


def make_hidden(counts, gate_up, pick):
    tokens, _, local = gate_up.shape
    rows = 128
    return pl.pallas_call(
        hidden_kernel,
        grid_spec=pltpu.PrefetchScalarGridSpec(
            num_scalar_prefetch=1,
            grid=(tokens // rows,),
            in_specs=[
                pl.BlockSpec((rows, 2, local), lambda i, c: (i, 0, 0)),
                pl.BlockSpec(pick.shape, lambda i, c: (0, 0)),
            ],
            out_specs=[
                pl.BlockSpec((rows, local), lambda i, c: (i, 0)),
                pl.BlockSpec((pick.shape[0], rows), lambda i, c: (0, i)),
            ],
        ),
        out_shape=[
            jax.ShapeDtypeStruct((tokens, local), jnp.bfloat16),
            jax.ShapeDtypeStruct((pick.shape[0], tokens), jnp.bfloat16),
        ],
        compiler_params=pltpu.CompilerParams(vmem_limit_bytes=48 << 20),
    )(counts, gate_up, pick)


def hessian_kernel(
    n, chunk, hidden_ref, own_ref, count_ref, hess_ref, cross_ref, total_ref,
    acts, part, core_out, core_in, line_out, line_in, done, cpart, cin, call,
    push_sem, fwd_sem, acts_sem, core_ssem, core_rsem, line_ssem, line_rsem,
    done_ssem, done_rsem, local_sem, cpart_ssem, cpart_rsem, call_ssem, call_rsem,
):
    chan, grp = lax.axis_index("chan"), lax.axis_index("grp")
    half = n // 2
    z, y = chan // 2, chan % 2
    line, core = grp // 2, grp % 2
    share, local = line_out.shape[1], line_out.shape[2]
    beside = {"chan": z * 2 + (1 - y)}
    other_core = {"grp": line * 2 + (1 - core)}
    other_line = {"grp": (1 - line) * 2 + core}

    barrier = pltpu.get_barrier_semaphore()

    def greet(j, _):
        pl.semaphore_signal(barrier, inc=1, device_id={"chan": (chan + j) % n}, device_id_type=MESH)
        return 0

    lax.fori_loop(1, n, greet, 0)
    for j in range(1, 4):
        pl.semaphore_signal(barrier, inc=1, device_id={"grp": (grp + j) % 4}, device_id_type=MESH)
    pl.semaphore_wait(barrier, n - 1 + 3)

    def remote(src, dst, ssem, rsem, where):
        return pltpu.make_async_remote_copy(
            src_ref=src, dst_ref=dst, send_sem=ssem, recv_sem=rsem,
            device_id=where, device_id_type=MESH)

    def block_at(k):
        return ((z + half - k // 2) % half) * 2 + (y + k) % 2

    def push(j):
        where = beside if j is None else {"chan": ((z + j) % half) * 2 + y}
        sem = push_sem.at[0 if j is None else j]
        return remote(own_ref, acts.at[chan], sem, acts_sem.at[chan], where)

    def forward(k):
        b = block_at(k)
        return remote(acts.at[b], acts.at[b], fwd_sem.at[k // 2], acts_sem.at[b], beside)

    def start_push(j, _):
        push(j).start()
        return 0

    def wait_push(j, _):
        push(j).wait_send()
        return 0

    push(None).start()
    lax.fori_loop(1, half, start_push, 0)
    keep = pltpu.make_async_copy(own_ref, acts.at[chan], local_sem.at[n])
    keep.start()
    keep.wait()

    def arrived(b):
        remote(own_ref, acts.at[b], push_sem.at[0], acts_sem.at[b], beside).wait_recv()

    def to_core(b):
        return remote(core_out.at[b], core_in.at[b], core_ssem.at[b], core_rsem.at[b], other_core)

    def to_line(b):
        return remote(line_out.at[b], line_in.at[b], line_ssem.at[b], line_rsem.at[b], other_line)

    def to_done(b):
        return remote(done.at[b], hess_ref.at[b, core], done_ssem.at[b], done_rsem.at[b], other_core)

    def from_done(b):
        return remote(done.at[b], hess_ref.at[b, 1 - core], done_ssem.at[b], done_rsem.at[b], other_core)

    def to_own(b):
        return pltpu.make_async_copy(done.at[b], hess_ref.at[b, core], local_sem.at[b])

    def product(k):
        b = block_at(k)
        left = acts[b].reshape(2 * share, acts.shape[3])

        def tile(t, _):
            at = pl.ds(pl.multiple_of(t * chunk, chunk), chunk)
            both = jnp.dot(left, hidden_ref[:, at], preferred_element_type=jnp.float32)
            low, high = both[:share], both[share:]
            part[k % 2, :, at] = jnp.where(core == 0, low, high)
            core_out[b, :, at] = jnp.where(core == 0, high, low).astype(jnp.bfloat16)
            return 0

        lax.fori_loop(0, local // chunk, tile, 0)
        to_core(b).start()

    def pair(k):
        b = block_at(k)
        to_core(b).wait_recv()

        def tile(t, _):
            at = pl.ds(pl.multiple_of(t * chunk, chunk), chunk)
            line_out[b, :, at] = (part[k % 2, :, at] + core_in[b, :, at].astype(jnp.float32)).astype(jnp.bfloat16)
            return 0

        lax.fori_loop(0, local // chunk, tile, 0)
        to_line(b).start()

    def finish(k):
        b = block_at(k)
        to_line(b).wait_recv()

        def tile(t, _):
            at = pl.ds(pl.multiple_of(t * chunk, chunk), chunk)
            done[b, :, at] = (
                line_out[b, :, at].astype(jnp.float32) + line_in[b, :, at].astype(jnp.float32)
            ).astype(jnp.bfloat16)
            return 0

        lax.fori_loop(0, local // chunk, tile, 0)
        to_done(b).start()
        to_own(b).start()

    def relay(h, _):
        arrived(block_at(2 * h))
        forward(2 * h).start()
        return 0

    product(0)
    arrived(block_at(1))
    product(1)
    pair(0)
    lax.fori_loop(1, half, relay, 0)
    pair(1)

    def gather(h, _):
        arrived(block_at(2 * h + 1))
        return 0

    def steps(k, _):
        product(k)
        pair(k - 1)
        finish(k - 2)
        return 0

    lax.fori_loop(1, half, gather, 0)

    first = acts[:, 0].reshape(n * share, acts.shape[3])
    cpart[:share] = lax.dot_general(acts[chan, 1], first, NT, preferred_element_type=jnp.float32)
    cpart[share:] = jnp.broadcast_to(count_ref[:, :1], (8, n * share))

    def to_group(j):
        return remote(cpart, cin.at[j - 1], cpart_ssem.at[j - 1], cpart_rsem.at[j - 1], {"grp": (grp + j) % 4})

    for j in range(1, 4):
        to_group(j).start()

    product(2)
    finish(0)
    lax.fori_loop(3, min(5, n), steps, 0)

    for j in range(1, 4):
        to_group(j).wait_recv()
    total = cpart[share:] + cin[0, share:] + cin[1, share:] + cin[2, share:]
    call[chan] = (cpart[:share] + cin[0, :share] + cin[1, :share] + cin[2, :share]) / total[:1]
    total_ref[...] = total[:, :128]

    def to_chan(j):
        return remote(call.at[chan], call.at[chan], call_ssem.at[j], call_rsem.at[chan], {"chan": (chan + j) % n})

    def start_chan(j, _):
        to_chan(j).start()
        return 0

    lax.fori_loop(1, n, start_chan, 0)
    lax.fori_loop(5, n, steps, 0)
    pair(n - 1)
    finish(n - 2)

    def end_chan(j, _):
        b = (chan + j) % n
        remote(call.at[chan], call.at[b], call_ssem.at[j], call_rsem.at[b], {"chan": b}).wait_recv()
        to_chan(j).wait_send()
        return 0

    lax.fori_loop(1, n, end_chan, 0)
    cross_ref[...] = call[...]
    finish(n - 1)

    push(None).wait_send()
    lax.fori_loop(1, half, wait_push, 0)
    for j in range(1, 4):
        to_group(j).wait_send()

    def end_forward(h, _):
        forward(2 * h).wait_send()
        return 0

    lax.fori_loop(1, half, end_forward, 0)

    def end_block(b, _):
        to_core(b).wait_send()
        to_line(b).wait_send()
        to_done(b).wait_send()
        from_done(b).wait_recv()
        to_own(b).wait()
        return 0

    lax.fori_loop(0, n, end_block, 0)


def make_hessian(n, hidden, own, count):
    tokens, local = hidden.shape
    share = own.shape[1]
    chunk = 512 if local % 512 == 0 else local
    vmem = pl.BlockSpec(memory_space=pltpu.VMEM)
    blocks = pltpu.VMEM((n, share, local), jnp.bfloat16)
    dma = pltpu.SemaphoreType.DMA
    return pl.pallas_call(
        functools.partial(hessian_kernel, n, chunk),
        in_specs=[vmem, vmem, vmem],
        out_specs=[pl.BlockSpec(memory_space=pl.ANY), vmem, vmem],
        out_shape=[
            jax.ShapeDtypeStruct((n, 2, share, local), jnp.bfloat16),
            jax.ShapeDtypeStruct((n, share, n * share), jnp.float32),
            jax.ShapeDtypeStruct((8, 128), jnp.float32),
        ],
        scratch_shapes=[
            pltpu.VMEM((n, 2, share, tokens), jnp.bfloat16),
            pltpu.VMEM((2, share, local), jnp.float32),
            blocks, blocks, blocks, blocks, blocks,
            pltpu.VMEM((share + 8, n * share), jnp.float32),
            pltpu.VMEM((3, share + 8, n * share), jnp.float32),
            pltpu.VMEM((n, share, n * share), jnp.float32),
            dma((n // 2,)), dma((n // 2,)), dma((n,)), dma((n,)), dma((n,)), dma((n,)), dma((n,)),
            dma((n,)), dma((n,)), dma((n + 1,)), dma((3,)), dma((3,)), dma((n,)), dma((n,)),
        ],
        compiler_params=pltpu.CompilerParams(
            collective_id=0, has_side_effects=True, vmem_limit_bytes=56 << 20
        ),
    )(hidden, own, count)


def body(gate_up, counts, panels, inverses, down_weight):
    tokens, _, local = gate_up.shape
    n = lax.axis_size("chan")
    share = panels.shape[1] // n
    columns = down_weight.shape[1]
    shard = lax.axis_index("chan")
    picked = lax.dynamic_slice(panels, (0, shard * share), (2, share)) - shard * local
    hits = picked.reshape(2 * share)[:, None] == jnp.arange(local, dtype=jnp.int32)[None, :]
    pick = hits.astype(jnp.bfloat16)
    kept = jnp.logical_not(jnp.any(hits, axis=0))
    rows = jnp.dot(pick, down_weight, preferred_element_type=jnp.float32).astype(jnp.bfloat16)
    rows = lax.all_gather(rows, "chan", axis=0, tiled=False).reshape(n, 2, share, columns)
    hidden, acts = make_hidden(counts, gate_up, pick)
    count = jnp.broadcast_to(counts.astype(jnp.float32)[:, None], (8, 128))
    hess, cross, total = make_hessian(n, hidden, acts.reshape(2, share, tokens), count)
    width = n * share
    high = lax.Precision.HIGH
    first_rows = rows[:, 0].reshape(width, columns).astype(jnp.float32)
    second_rows = rows[:, 1].reshape(width, columns).astype(jnp.float32)
    first = jnp.dot(inverses[0], first_rows, precision=high)
    second = second_rows - jnp.dot(cross.reshape(width, width), first, precision=high)
    second = jnp.dot(inverses[1], second, precision=high)
    update = jnp.stack((first.reshape(n, share, columns), second.reshape(n, share, columns)), axis=1)
    update = (update / total[0, 0]).astype(jnp.bfloat16).reshape(2 * width, columns)
    change = lax.dot_general(
        hess.reshape(2 * width, local), update, (((0,), (0,)), ((), ())), preferred_element_type=jnp.float32
    )
    weight = jnp.where(kept[:, None], down_weight.astype(jnp.float32) - change, 0.0)
    return weight.astype(jnp.bfloat16)


def solution(mesh):
    in_specs = (P("grp", None, "chan"), P("grp"), P(), P(), P("chan", "grp"))
    out_specs = P("chan", "grp")
    return jax.shard_map(body, mesh=mesh, in_specs=in_specs, out_specs=out_specs, check_vma=False)
```

time: 783 us -> 217 us (0.28); the launches traced: 773 us -> 215 us
  waiting for transfers between devices: 399 us -> 0.02 us
  local copies, waits for them, and re-layouts: 160 us -> 5.46 us
  Pallas kernels: 0 us -> 147 us
  matrix products: 145 us -> 46.9 us
  other arithmetic: 46.9 us -> 1.25 us
    psum x1 -> x0, waiting for transfers between devices: 239 us -> none  [body(): lax.psum((first_part, second_part, counts[0].astype(jnp.float32)), 'grp')]
    all_gather x5 -> x1, waiting for transfers between devices: 160 us -> 0.01 us  [body(): lax.all_gather(rows, 'chan', axis=0, tiled=False)]
    pallas_call x0 -> x2, Pallas kernels: none -> 147 us  [the longest x1 133 us: make_hessian(): pl.pallas_call(functools.partial(hessian_kernel, n, chunk), in_specs=[vme...]
    dot_general x6 -> x5, matrix products: 145 us -> 46.9 us  [the longest x1 27.1 us: body(): lax.dot_general(hess.reshape(2 * width, local), update, (((0,), (0,)), ((...]
    unnamed x6 -> x16, local copies, waits for them, and re-layouts: 61.3 us -> 0.75 us
    scatter x2 -> x0, local copies, waits for them, and re-layouts: 39.8 us -> none  [the longest x1 19.9 us: body(): weight_state = weight_state.at[picked[0]].set(0.0)]
    gather x5 -> x0, local copies, waits for them, and re-layouts: 29.6 us -> none  [the longest x1 8.09 us: body(): jnp.take(down_weight, picked[1], axis=0)]
    convert_element_type x3 -> x0, other arithmetic: 26.9 us -> none  [the longest x1 16.5 us: body(): return weight_state.astype(jnp.bfloat16)]
  transfers between devices with their start and end apart: 6 -> 1, of which waited for: 6 -> 0; matrix products, arithmetic and copies ran while one was open for 9% -> 1% of each run, Pallas kernels for 0% -> 68%
where the time goes in v1:
time: 217 us; the launch traced here: 215 us
  Pallas kernels  147 us (68%)
  matrix products  46.9 us (22%)
  between operations  14.2 us (7%)
  local copies, waits for them, and re-layouts  5.46 us (3%)
    pallas_call x1, Pallas kernels, make_hessian(): pl.pallas_call(functools.partial(hessian_kernel, n, chunk), in_specs=[vme...  133 us
    dot_general x1, matrix products, body(): lax.dot_general(hess.reshape(2 * width, local), update, (((0,), (0,)), ((...  27.1 us
    pallas_call x1, Pallas kernels, make_hidden(): pl.pallas_call(hidden_kernel, grid_spec=pltpu.PrefetchScalarGridSpec(num_...  14.1 us
    dot_general x1, matrix products, body(): jnp.dot(pick, down_weight, preferred_element_type=jnp.float32)  8.12 us
    dot_general x1, matrix products, body(): second = jnp.dot(inverses[1], second, precision=high)  5.31 us
  transfers between devices with their start and end apart: 1, of which 0 were waited for; matrix products, arithmetic and copies ran while one was open for 1% of the time, Pallas kernels for 68%

profile of v1, /device:TPU:26, one launch (start us, length us, event | category | flops | bytes accessed | tf_op | source)
XLA Modules:
  0.0 214.7 jit_solution(14036914586028848202)
XLA Ops:
  6.5 0.0 all-gather.3.cloned.1.call-start
  6.5 0.8 dynamic-slice_subtract_fusion
  7.3 0.1 eq.15
  7.4 8.1 %convolution_convert_fusion = bf16[128,2048]{1,0:T(8,128)(2,1)} fusion(bf16[3584,2048]{1,0:T(8,128)(2,1)} %param.9, s32[128]{0:T(128)S(1)} %eq.15), kind=kOutput, calls=%fused_computation.8 | convolution fusion | flops 1879769088 | bytes 15204864 | tf_op jit(solution)/shard_map/dot_general | solution.py:302
  15.5 0.0 all-gather.3.cloned.1.call-update
  16.2 0.5 fusion.7
  16.7 14.1 %shard_map.55 = (bf16[1024,3584]{1,0:T(8,128)(2,1)}, bf16[128,1024]{1,0:T(8,128)(2,1)S(1)}) custom-call(s32[1]{0:T(128)S(6)} %copy.9.count_ref, bf16[1024,2,3584]{2,1,0:T(2,128)(2,1)} %x_ref.1, bf16[128,3584]{1,0:T(8,128)(2,1)S(1)} %get-tuple-element.18.pick_ref), custom_call_target="tpu_custom_call" | custom-call | tf_op jit(solution)/shard_map/pallas_call | solution.py:33
  30.8 0.7 copy-done
  31.5 0.6 broadcast_in_dim.24.count_ref
  32.1 132.8 %shard_map.56 = (bf16[8,2,64,3584]{3,2,1,0:T(8,128)(2,1)}, f32[8,64,512]{2,1,0:T(8,128)}, f32[8,128]{1,0:T(8,128)}) custom-call(bf16[1024,3584]{1,0:T(8,128)(2,1)} %get-tuple-element.10.hidden_ref, bf16[2,64,1024]{2,1,0:T(8,128)(2,1)} %bitcast.37, f32[8,128]{1,0:T(8,128)} %broadcast_in_dim.24.count_ref), custom_call_target="tpu_custom_call" | custom-call | tf_op jit(solution)/shard_map/pallas_call | solution.py:267
  164.9 1.2 slice.19
  166.0 2.9 %fusion.15 = (bf16[8,1,64,2048]{3,2,1,0:T(8,128)(2,1)S(1)}, bf16[8,1,64,2048]{3,2,1,0:T(8,128)(2,1)S(1)}) fusion(bf16[8,2,64,2048]{3,2,1,0:T(8,128)(2,1)} %bitcast.43), kind=kLoop, calls=%fused_computation.20 | loop fusion | bytes 8388608 | tf_op jit(solution)/shard_map/slice | solution.py:310
  168.9 0.0 copy-done.2
  168.9 0.0 copy-start.3
  168.9 0.0 slice-start
  168.9 0.0 slice-start.1
  168.9 2.5 %fusion.9 = f32[2048,512]{0,1:T(8,128)S(1)} fusion(bf16[512,2048]{1,0:T(8,128)(2,1)S(1)} %bitcast.41, f32[2,512,512]{2,1,0:T(8,128)S(1)} %copy-done.2), kind=kOutput, calls=%fused_computation.13 | convolution fusion | flops 3221225472 | bytes 7340032 | tf_op jit(solution)/shard_map/dot_general | solution.py:311
  171.5 0.0 copy-start.1
  171.5 0.0 slice-start.2
  171.5 3.9 %fusion.16 = f32[512,2048]{1,0:T(8,128)S(1)} fusion(f32[512,512]{1,0:T(8,128)S(1)} %bitcast.45, f32[2048,512]{0,1:T(8,128)S(1)} %fusion.9), kind=kOutput, calls=%fused_computation.21 | convolution fusion | flops 3221225472 | bytes 9437184 | tf_op jit(solution)/shard_map/dot_general | solution.py:312
  175.4 0.0 slice-start.3
  175.4 5.3 %fusion.4 = f32[2048,512]{0,1:T(8,128)} fusion(f32[512,2048]{1,0:T(8,128)S(1)} %fusion.16, bf16[512,2048]{1,0:T(8,128)(2,1)S(1)} %bitcast.42, f32[2,512,512]{2,1,0:T(8,128)S(1)} %copy-done.2), kind=kOutput, calls=%fused_computation.6 | convolution fusion | flops 3223322624 | bytes 11534336 | tf_op jit(solution)/shard_map/dot_general | solution.py:313
  180.7 0.0 slice-done.1
  180.7 27.1 %fusion.1 = bf16[3584,2048]{1,0:T(8,128)(2,1)} fusion(bf16[3584,2048]{1,0:T(8,128)(2,1)S(1)} %bitcast.39, bf16[8,2,64,3584]{3,2,1,0:T(8,128)(2,1)} %get-tuple-element.12, pred[3584]{0:T(1024)(128)(4,1)S(1)} %not.7, f32[8,1,64,2048]{3,2,1,0:T(8,128)} %bitcast.44, f32[8,1,64,2048]{3,2,1,0:T(8,128)} %bitcast.40, f32[]{:T(128)} %bitcast.14), kind=kOutput, calls=%fused_computation.2 | convolution fusion | flops 15068037120 | bytes 45092356 | tf_op jit(solution)/shard_map/dot_general | solution.py:316
  (10 shorter events, 0.0 us)
Async XLA Ops:
  6.5 159.5 %all-gather.3.cloned.1.call-start = ((), (), s32[]{:S(2)}) async-start(), calls=%async_computation | async-start | bytes 4718592 | tf_op jit(solution)/shard_map/all_gather | solution.py:303
  30.8 0.7 copy-start
  166.0 2.9 %copy-start.2 = (f32[2,512,512]{2,1,0:T(8,128)S(1)}, f32[2,512,512]{2,1,0:T(8,128)}, u32[]{:S(2)}) copy-start(f32[2,512,512]{2,1,0:T(8,128)} %param.8) | copy-start | bytes 6291460
  168.9 2.6 %copy-start.3 = (f32[8,64,512]{2,1,0:T(8,128)S(1)}, f32[8,64,512]{2,1,0:T(8,128)}, u32[]{:S(2)}) copy-start(f32[8,64,512]{2,1,0:T(8,128)} %get-tuple-element.13) | copy-start | bytes 3145732
  168.9 11.8 %slice-start = ((s8[14680064]{0:T(1024)(128)(4,1)}), s8[4194304]{0:T(1024)(128)(4,1)S(1)}, s32[]{:S(2)}) async-start(s8[14680064]{0:T(1024)(128)(4,1)} %bitcast.38), calls=%async_computation.1 | async-start | bytes 8388608
  168.9 11.8 %slice-start.1 = ((s8[14680064]{0:T(1024)(128)(4,1)}), s8[4194304]{0:T(1024)(128)(4,1)S(1)}, s32[]{:S(2)}) async-start(s8[14680064]{0:T(1024)(128)(4,1)} %bitcast.38), calls=%async_computation.2 | async-start | bytes 8388608
  171.5 3.9 %copy-start.1 = (f32[2048,512]{0,1:T(8,128)}, f32[2048,512]{0,1:T(8,128)S(1)}, u32[]{:S(2)}) copy-start(f32[2048,512]{0,1:T(8,128)S(1)} %fusion.9) | copy-start | bytes 12582916
  171.5 9.2 %slice-start.2 = ((s8[14680064]{0:T(1024)(128)(4,1)}), s8[4194304]{0:T(1024)(128)(4,1)S(1)}, s32[]{:S(2)}) async-start(s8[14680064]{0:T(1024)(128)(4,1)} %bitcast.38), calls=%async_computation.3 | async-start | bytes 8388608
  175.4 5.3 %slice-start.3 = ((s8[14680064]{0:T(1024)(128)(4,1)}), s8[2097152]{0:T(1024)(128)(4,1)S(1)}, s32[]{:S(2)}) async-start(s8[14680064]{0:T(1024)(128)(4,1)} %bitcast.38), calls=%async_computation.4 | async-start | bytes 4194304
Sparse Core Ops, SparseCore 0:
  15.6 95.7 all-gather.2

commit v2 on v1

--- a/solution.py
+++ b/solution.py
@@ -53,10 +53,11 @@
 
 
 def hessian_kernel(
-    n, chunk, hidden_ref, own_ref, count_ref, hess_ref, cross_ref, total_ref,
+    n, chunk, hidden_ref, own_ref, count_ref, rows_ref, hess_ref, cross_ref, total_ref, all_rows_ref,
     acts, part, core_out, core_in, line_out, line_in, done, cpart, cin, call,
     push_sem, fwd_sem, acts_sem, core_ssem, core_rsem, line_ssem, line_rsem,
     done_ssem, done_rsem, local_sem, cpart_ssem, cpart_rsem, call_ssem, call_rsem,
+    row_push, row_fwd, row_sem, row_local,
 ):
     chan, grp = lax.axis_index("chan"), lax.axis_index("grp")
     half = n // 2
@@ -174,24 +175,63 @@
         forward(2 * h).start()
         return 0
 
+    def gather(h, _):
+        arrived(block_at(2 * h + 1))
+        return 0
+
+    def steps(k, _):
+        product(k)
+        pair(k - 1)
+        finish(k - 2)
+        return 0
+
+    def rows_push(j):
+        where = beside if j is None else {"chan": ((z + j) % half) * 2 + y}
+        sem = row_push.at[0 if j is None else j]
+        return remote(rows_ref, all_rows_ref.at[chan], sem, row_sem.at[chan], where)
+
+    def rows_arrived(b):
+        remote(rows_ref, all_rows_ref.at[b], row_push.at[0], row_sem.at[b], beside).wait_recv()
+
+    def rows_forward(h):
+        b = block_at(2 * h)
+        return remote(all_rows_ref.at[b], all_rows_ref.at[b], row_fwd.at[h], row_sem.at[b], beside)
+
+    def start_rows(j, _):
+        rows_push(j).start()
+        return 0
+
+    def relay_rows(h, _):
+        rows_arrived(block_at(2 * h))
+        rows_forward(h).start()
+        return 0
+
+    def end_rows(h, _):
+        rows_arrived(block_at(2 * h + 1))
+        return 0
+
+    def end_push(h, _):
+        rows_push(h).wait_send()
+        rows_forward(h).wait_send()
+        return 0
+
     product(0)
     arrived(block_at(1))
     product(1)
     pair(0)
-    lax.fori_loop(1, half, relay, 0)
+    lax.fori_loop(1, 2, relay, 0)
+    product(2)
     pair(1)
-
-    def gather(h, _):
-        arrived(block_at(2 * h + 1))
-        return 0
-
-    def steps(k, _):
-        product(k)
-        pair(k - 1)
-        finish(k - 2)
-        return 0
-
-    lax.fori_loop(1, half, gather, 0)
+    arrived(block_at(3))
+    product(3)
+    pair(2)
+    lax.fori_loop(2, half, relay, 0)
+    finish(0)
+    lax.fori_loop(2, half, gather, 0)
+    rows_push(None).start()
+    lax.fori_loop(1, half, start_rows, 0)
+    keep_rows = pltpu.make_async_copy(rows_ref, all_rows_ref.at[chan], row_local)
+    keep_rows.start()
 
     first = acts[:, 0].reshape(n * share, acts.shape[3])
     cpart[:share] = lax.dot_general(acts[chan, 1], first, NT, preferred_element_type=jnp.float32)
@@ -203,9 +243,8 @@
     for j in range(1, 4):
         to_group(j).start()
 
-    product(2)
-    finish(0)
-    lax.fori_loop(3, min(5, n), steps, 0)
+    finish(1)
+    lax.fori_loop(4, 5, steps, 0)
 
     for j in range(1, 4):
         to_group(j).wait_recv()
@@ -221,7 +260,15 @@
         return 0
 
     lax.fori_loop(1, n, start_chan, 0)
-    lax.fori_loop(5, n, steps, 0)
+    def late_steps(k, _):
+        steps(k, 0)
+        relay_rows(k - 4, 0)
+        return 0
+
+    middle = max(5, min(half + 4, n))
+    lax.fori_loop(5, middle, late_steps, 0)
+    lax.fori_loop(middle, n, steps, 0)
+    lax.fori_loop(middle - 4, half, relay_rows, 0)
     pair(n - 1)
     finish(n - 2)
 
@@ -234,6 +281,10 @@
     lax.fori_loop(1, n, end_chan, 0)
     cross_ref[...] = call[...]
     finish(n - 1)
+    lax.fori_loop(0, half, end_rows, 0)
+    rows_push(None).wait_send()
+    lax.fori_loop(1, half, end_push, 0)
+    keep_rows.wait()
 
     push(None).wait_send()
     lax.fori_loop(1, half, wait_push, 0)
@@ -257,7 +308,7 @@
     lax.fori_loop(0, n, end_block, 0)
 
 
-def make_hessian(n, hidden, own, count):
+def make_hessian(n, hidden, own, count, rows):
     tokens, local = hidden.shape
     share = own.shape[1]
     chunk = 512 if local % 512 == 0 else local
@@ -266,12 +317,13 @@
     dma = pltpu.SemaphoreType.DMA
     return pl.pallas_call(
         functools.partial(hessian_kernel, n, chunk),
-        in_specs=[vmem, vmem, vmem],
-        out_specs=[pl.BlockSpec(memory_space=pl.ANY), vmem, vmem],
+        in_specs=[vmem, vmem, vmem, vmem],
+        out_specs=[pl.BlockSpec(memory_space=pl.ANY), vmem, vmem, pl.BlockSpec(memory_space=pl.ANY)],
         out_shape=[
             jax.ShapeDtypeStruct((n, 2, share, local), jnp.bfloat16),
             jax.ShapeDtypeStruct((n, share, n * share), jnp.float32),
             jax.ShapeDtypeStruct((8, 128), jnp.float32),
+            jax.ShapeDtypeStruct((n,) + rows.shape, jnp.bfloat16),
         ],
         scratch_shapes=[
             pltpu.VMEM((n, 2, share, tokens), jnp.bfloat16),
@@ -282,11 +334,69 @@
             pltpu.VMEM((n, share, n * share), jnp.float32),
             dma((n // 2,)), dma((n // 2,)), dma((n,)), dma((n,)), dma((n,)), dma((n,)), dma((n,)),
             dma((n,)), dma((n,)), dma((n + 1,)), dma((3,)), dma((3,)), dma((n,)), dma((n,)),
+            dma((n // 2,)), dma((n // 2,)), dma((n,)), dma(()),
         ],
         compiler_params=pltpu.CompilerParams(
             collective_id=0, has_side_effects=True, vmem_limit_bytes=56 << 20
         ),
-    )(hidden, own, count)
+    )(hidden, own, count, rows)
+
+
+def compensate_kernel(
+    hess_ref, cross_ref, total_ref, rows_ref, inverses_ref, weight_ref, kept_ref, out_ref, update_ref
+):
+    n, _, share, columns = rows_ref.shape
+    width = n * share
+    step = min(512, columns)
+    spans = [slice(t * step, (t + 1) * step) for t in range(columns // step)]
+
+    def dot(a, b):
+        return jnp.dot(a, b, preferred_element_type=jnp.float32)
+
+    @pl.when(pl.program_id(0) == 0)
+    def _():
+        top = inverses_ref[0]
+        coarse = top.astype(jnp.bfloat16)
+        fine = (top - coarse.astype(jnp.float32)).astype(jnp.bfloat16)
+        low = inverses_ref[1].astype(jnp.bfloat16)
+        cross = cross_ref[...].reshape(width, width).astype(jnp.bfloat16)
+        scale = 1.0 / total_ref[:1, :1]
+        for at in spans:
+            rows = rows_ref[:, 0, :, at].reshape(width, step)
+            first = dot(coarse, rows) + dot(fine, rows)
+            second = rows_ref[:, 1, :, at].reshape(width, step).astype(jnp.float32)
+            second = dot(low, (second - dot(cross, first.astype(jnp.bfloat16))).astype(jnp.bfloat16))
+            update_ref[:, 0, :, at] = (first * scale).reshape(n, share, step).astype(jnp.bfloat16)
+            update_ref[:, 1, :, at] = (second * scale).reshape(n, share, step).astype(jnp.bfloat16)
+
+    left = hess_ref[...].reshape(2 * width, hess_ref.shape[3]).T
+    kept = kept_ref[...] > 0.5
+    for at in spans:
+        change = dot(left, update_ref[:, :, :, at].reshape(2 * width, step))
+        out_ref[:, at] = jnp.where(kept, weight_ref[:, at].astype(jnp.float32) - change, 0.0).astype(jnp.bfloat16)
+
+
+def compensate(hess, cross, total, rows, inverses, weight, kept):
+    local, columns = weight.shape
+    block = 256 if local % 256 == 0 else local
+
+    def whole(array):
+        return pl.BlockSpec(array.shape, lambda i: (0,) * array.ndim)
+
+    return pl.pallas_call(
+        compensate_kernel,
+        grid=(local // block,),
+        in_specs=[
+            pl.BlockSpec(hess.shape[:3] + (block,), lambda i: (0, 0, 0, i)),
+            whole(cross), whole(total), whole(rows), whole(inverses),
+            pl.BlockSpec((block, columns), lambda i: (i, 0)),
+            pl.BlockSpec((block, 1), lambda i: (i, 0)),
+        ],
+        out_specs=pl.BlockSpec((block, columns), lambda i: (i, 0)),
+        out_shape=jax.ShapeDtypeStruct(weight.shape, jnp.bfloat16),
+        scratch_shapes=[pltpu.VMEM(rows.shape, jnp.bfloat16)],
+        compiler_params=pltpu.CompilerParams(vmem_limit_bytes=56 << 20),
+    )(hess, cross, total, rows, inverses, weight, kept.astype(jnp.float32)[:, None])
 
 
 def body(gate_up, counts, panels, inverses, down_weight):
@@ -300,24 +410,12 @@
     pick = hits.astype(jnp.bfloat16)
     kept = jnp.logical_not(jnp.any(hits, axis=0))
     rows = jnp.dot(pick, down_weight, preferred_element_type=jnp.float32).astype(jnp.bfloat16)
-    rows = lax.all_gather(rows, "chan", axis=0, tiled=False).reshape(n, 2, share, columns)
     hidden, acts = make_hidden(counts, gate_up, pick)
     count = jnp.broadcast_to(counts.astype(jnp.float32)[:, None], (8, 128))
-    hess, cross, total = make_hessian(n, hidden, acts.reshape(2, share, tokens), count)
-    width = n * share
-    high = lax.Precision.HIGH
-    first_rows = rows[:, 0].reshape(width, columns).astype(jnp.float32)
-    second_rows = rows[:, 1].reshape(width, columns).astype(jnp.float32)
-    first = jnp.dot(inverses[0], first_rows, precision=high)
-    second = second_rows - jnp.dot(cross.reshape(width, width), first, precision=high)
-    second = jnp.dot(inverses[1], second, precision=high)
-    update = jnp.stack((first.reshape(n, share, columns), second.reshape(n, share, columns)), axis=1)
-    update = (update / total[0, 0]).astype(jnp.bfloat16).reshape(2 * width, columns)
-    change = lax.dot_general(
-        hess.reshape(2 * width, local), update, (((0,), (0,)), ((), ())), preferred_element_type=jnp.float32
+    hess, cross, total, rows = make_hessian(
+        n, hidden, acts.reshape(2, share, tokens), count, rows.reshape(2, share, columns)
     )
-    weight = jnp.where(kept[:, None], down_weight.astype(jnp.float32) - change, 0.0)
-    return weight.astype(jnp.bfloat16)
+    return compensate(hess, cross, total, rows, inverses, down_weight, kept)
 
 
 def solution(mesh):

time: 217 us -> 182 us (0.84)
  matrix products: 46.9 us -> 8.08 us
  Pallas kernels: 147 us -> 168 us
  between operations: 14.2 us -> 0.67 us
  local copies, waits for them, and re-layouts: 5.46 us -> 3.25 us
    dot_general x4 -> x0, matrix products: 38.8 us -> none  [the longest x1 27.1 us: body(): lax.dot_general(hess.reshape(2 * width, local), update, (((0,), (0,)), ((...]
    pallas_call x0 -> x1, Pallas kernels: none -> 31.7 us  [compensate(): pl.pallas_call(compensate_kernel, grid=(local // block,), in_specs=[pl.Bl...]
    pallas_call x1, Pallas kernels: 133 us -> 123 us  [make_hessian(): pl.pallas_call(functools.partial(hessian_kernel, n, chunk), in_specs=[vme...]
    slice x2 -> x0, local copies, waits for them, and re-layouts: 4.04 us -> none  [the longest x1 2.88 us: body(): second_rows = rows[:, 1].reshape(width, columns).astype(jnp.float32)]
  transfers between devices with their start and end apart: 1 -> 0, of which waited for: 0 -> 0; matrix products, arithmetic and copies ran while one was open for 1% -> 0% of each run, Pallas kernels for 68% -> 0%
where the time goes in v2:
time: 182 us; the launch traced here: 181 us
  Pallas kernels  168 us (92%)
  matrix products  8.08 us (4%)
  local copies, waits for them, and re-layouts  3.25 us (2%)
    pallas_call x1, Pallas kernels, make_hessian(): pl.pallas_call(functools.partial(hessian_kernel, n, chunk), in_specs=[vme...  123 us
    pallas_call x1, Pallas kernels, compensate(): pl.pallas_call(compensate_kernel, grid=(local // block,), in_specs=[pl.Bl...  31.7 us
    pallas_call x1, Pallas kernels, make_hidden(): pl.pallas_call(hidden_kernel, grid_spec=pltpu.PrefetchScalarGridSpec(num_...  13.7 us
    dot_general x1, matrix products, body(): jnp.dot(pick, down_weight, preferred_element_type=jnp.float32)  8.08 us

profile of v2, /device:TPU:26, one launch (start us, length us, event | category | flops | bytes accessed | tf_op | source)
XLA Modules:
  0.0 181.5 jit_solution(4478330663223524845)
XLA Ops:
  0.7 0.8 dynamic-slice_subtract_fusion
  1.4 0.1 eq.15
  1.5 0.6 broadcast_in_dim.5.count_ref
  2.1 8.1 %convolution_convert_fusion = bf16[128,2048]{1,0:T(8,128)(2,1)} fusion(bf16[3584,2048]{1,0:T(8,128)(2,1)} %weight_ref.1, s32[128]{0:T(128)S(1)} %eq.15), kind=kOutput, calls=%fused_computation | convolution fusion | flops 1879769088 | bytes 15204864 | tf_op jit(solution)/shard_map/dot_general | solution.py:412
  10.2 0.5 fusion
  10.7 1.9 %reshape.24.kept_ref = f32[3584,1]{1,0:T(8,128)} reshape(f32[3584]{0:T(1024)S(1)} %not_convert_fusion) | data formatting | bytes 28672 | tf_op jit(solution)/shard_map/convert_element_type | solution.py:399
  12.5 13.7 %shard_map.55 = (bf16[1024,3584]{1,0:T(8,128)(2,1)}, bf16[128,1024]{1,0:T(8,128)(2,1)S(1)}) custom-call(s32[1]{0:T(128)S(6)} %copy.7.count_ref, bf16[1024,2,3584]{2,1,0:T(2,128)(2,1)} %x_ref.1, bf16[128,3584]{1,0:T(8,128)(2,1)S(1)} %get-tuple-element.18.pick_ref), custom_call_target="tpu_custom_call" | custom-call | tf_op jit(solution)/shard_map/pallas_call | solution.py:33
  26.3 0.0 copy-start
  26.3 0.7 copy-done
  27.0 122.8 %shard_map.56 = (bf16[8,2,64,3584]{3,2,1,0:T(8,128)(2,1)}, f32[8,64,512]{2,1,0:T(8,128)}, f32[8,128]{1,0:T(8,128)}, bf16[8,2,64,2048]{3,2,1,0:T(8,128)(2,1)}) custom-call(bf16[1024,3584]{1,0:T(8,128)(2,1)} %get-tuple-element.11.hidden_ref, bf16[2,64,1024]{2,1,0:T(8,128)(2,1)} %bitcast.4, f32[8,128]{1,0:T(8,128)} %broadcast_in_dim.5.count_ref, ...), custom_call_target="tpu_custom_call" | custom-call | tf_op jit(solution)/shard_map/pallas_call | solution.py:318
  149.8 31.7 %shard_map.57 = bf16[3584,2048]{1,0:T(8,128)(2,1)} custom-call(bf16[8,2,64,3584]{3,2,1,0:T(8,128)(2,1)} %get-tuple-element.13.hess_ref, f32[8,64,512]{2,1,0:T(8,128)} %get-tuple-element.14.cross_ref, f32[8,128]{1,0:T(8,128)} %get-tuple-element.15.total_ref, bf16[8,2,64,2048]{3,2,1,0:T(8,128)(2,1)} %get-tuple-element.16.rows_ref, ...), custom_call_target="tpu_custom_call" | custom-call | tf_op jit(solution)/shard_map/pallas_call | solution.py:386
  (1 shorter events, 0.0 us)
Async XLA Ops:
  26.3 0.7 copy-start
